TPU v7x, 256 devices: a whole 4x4x8 slice. The times are simulated.
256 devices in a mesh: dom: 64 (over x, z, core), loop: 4 (over y).
Axes of the slice: x: 4, y: 4, z: 8, core: 2. Of those that a mesh axis runs over, the one named last changes fastest.
Arguments:
- node_rows: bfloat16 [131072, 512], P(('dom', 'loop')), may hold values from -24 to 24
- w_dst: bfloat16 [512, 512], replicated, may hold values from -0.25 to 0.25
- w_src: bfloat16 [512, 512], replicated, may hold values from -0.25 to 0.25
- w_val: bfloat16 [512, 512], replicated, may hold values from -0.25 to 0.25
- w_query: bfloat16 [512, 512], replicated, may hold values from -0.25 to 0.25
- w_key: bfloat16 [512, 512], replicated, may hold values from -0.25 to 0.25
- w_value: bfloat16 [512, 512], replicated, may hold values from -0.25 to 0.25
- w_out: bfloat16 [512, 512], replicated, may hold values from -0.25 to 0.25
- norm_gain: float32 [512], replicated, may hold values from 0.5 to 1.5
- send_rows: int32 [64, 4, 64, 32], P('dom', 'loop'), may hold values from 0 to 511
- dst_rows: int32 [64, 4, 64, 32], P('dom', 'loop'), may hold values from 0 to 511
- counts: int32 [64, 4, 64], P('dom', 'loop'), may hold values from 1 to 32, as said below
- batch_ids: int32 [64, 2048], P('dom', 'loop'), may hold values from 0 to 1, never falling along the last dimension, each value on 1 to 1536 neighbouring positions
Outputs:
- layer_out: bfloat16 [131072, 512], P(('dom', 'loop'))
Inputs may be any that keep to these rules, and one draw needn't show every extreme that they name: `counts`: every device receives a full block of 32 live slots from some partition. `batch_ids`: each partition's nodes form two contiguous batches, each of 512 to 1536 nodes.
All inputs are finite; a program needn't handle non-finite values.
Results may differ from a plain program's by a relative error of at most 0.012.
The roundings to bfloat16 on the way count: a program that leaves them out, or rounds other values in their place, can miss the bound.
Values may be sent and summed in bfloat16 or wider, within the bound.
A program may use at most 128 MiB of HBM per device.

v0:
```python
import math

import jax
import jax.numpy as jnp
from jax import lax
from jax.sharding import PartitionSpec as P

D = 512
HEADS = 8
HEAD_DIM = 64


def per_device(
    node_rows,
    w_dst,
    w_src,
    w_val,
    w_query,
    w_key,
    w_value,
    w_out,
    norm_gain,
    send_rows,
    dst_rows,
    counts,
    batch_ids,
):
    local_rows = node_rows.shape[0]
    peers = send_rows.shape[2]
    slots = send_rows.shape[3]
    dst_term = jnp.dot(node_rows, w_dst, preferred_element_type=jnp.float32)
    selected = send_rows[0, 0].reshape(-1)
    weight_pair = jnp.concatenate([w_src, w_val], axis=1)
    projected = jnp.dot(node_rows, weight_pair, preferred_element_type=jnp.float32).astype(
        jnp.bfloat16
    )
    outgoing = jnp.take(projected, selected, axis=0).reshape(peers, slots, 2 * D)
    incoming = lax.all_to_all(outgoing, "dom", split_axis=0, concat_axis=0, tiled=True).reshape(
        peers * slots, 2 * D
    )
    edge_src = incoming[:, :D]
    edge_val = incoming[:, D:]
    targets = dst_rows[0, 0].reshape(-1)
    live_slot = (jnp.arange(slots, dtype=jnp.int32)[None, :] < counts[0, 0][:, None]).reshape(-1)
    gates = jax.nn.sigmoid(jnp.take(dst_term, targets, axis=0) + edge_src.astype(jnp.float32))
    gates = jnp.where(live_slot[:, None], gates, 0.0)
    onehot = (jnp.arange(local_rows, dtype=jnp.int32)[:, None] == targets[None, :]).astype(
        jnp.float32
    )
    stacked = jnp.concatenate([gates * edge_val.astype(jnp.float32), gates], axis=1)
    sums = jnp.dot(
        onehot, stacked, preferred_element_type=jnp.float32, precision=lax.Precision.HIGHEST
    )
    aggregated = sums[:, :D] / (1.0 + sums[:, D:])
    queries = (
        jnp.dot(node_rows, w_query, preferred_element_type=jnp.float32)
        .astype(jnp.bfloat16)
        .reshape(local_rows, HEADS, HEAD_DIM)
    )
    own_ids = batch_ids.reshape(-1)
    scale_factor = 1.0 / math.sqrt(HEAD_DIM)
    key_rows = jnp.dot(node_rows, w_key, preferred_element_type=jnp.float32).astype(jnp.bfloat16)
    value_rows = jnp.dot(node_rows, w_value, preferred_element_type=jnp.float32).astype(
        jnp.bfloat16
    )
    running = jnp.full((HEADS, local_rows), -1e30, jnp.float32)
    accumulated = jnp.zeros((local_rows, HEADS, HEAD_DIM), jnp.float32)
    key_heads = lax.all_gather(key_rows, "loop", axis=0, tiled=True).reshape(-1, HEADS, HEAD_DIM)
    value_heads = lax.all_gather(value_rows, "loop", axis=0, tiled=True).reshape(
        -1, HEADS, HEAD_DIM
    )
    scores = (
        jnp.einsum("qhd,khd->hqk", queries, key_heads, preferred_element_type=jnp.float32)
        * scale_factor
    )
    matching = own_ids[:, None] == lax.all_gather(own_ids, "loop", axis=0, tiled=True)[None, :]
    scores = jnp.where(matching[None], scores, -1e30)
    updated = jnp.maximum(running, jnp.max(scores, axis=-1))
    weights = jnp.where(matching[None], jnp.exp(scores - updated[:, :, None]), 0.0)
    shrink = jnp.exp(running - updated)
    weight_sum = jnp.sum(weights, axis=-1)
    contrib = jnp.einsum(
        "hqk,khd->qhd",
        weights.astype(jnp.bfloat16),
        value_heads,
        preferred_element_type=jnp.float32,
    )
    accumulated = accumulated * shrink.T[:, :, None] + contrib
    finished = (updated, weight_sum, accumulated)
    weight_sum = finished[1]
    accumulated = finished[2]
    mixed = (accumulated / weight_sum.T[:, :, None]).reshape(local_rows, D).astype(jnp.bfloat16)
    attended = jnp.dot(mixed, w_out, preferred_element_type=jnp.float32)
    total = node_rows.astype(jnp.float32) + aggregated + attended
    spread = jnp.sqrt(jnp.mean(total * total, axis=-1, keepdims=True) + 1e-06)
    return (total / spread * norm_gain).astype(jnp.bfloat16)


def solution(mesh):
    return jax.shard_map(
        per_device,
        mesh=mesh,
        in_specs=(
            P(("dom", "loop"), None),
            P(),
            P(),
            P(),
            P(),
            P(),
            P(),
            P(),
            P(),
            P("dom", "loop", None, None),
            P("dom", "loop", None, None),
            P("dom", "loop", None),
            P("dom", "loop"),
        ),
        out_specs=P(("dom", "loop"), None),
        check_vma=False,
    )
```

profile of v0, /device:TPU:1, one launch (start us, length us, event | category | flops | bytes accessed | tf_op | source)
XLA Modules:
  0.0 158.3 jit_solution(5162603818347855917)
XLA Ops:
  6.5 0.0 copy-start
  6.5 0.0 copy-start.1
  6.5 0.0 copy-start.4
  6.5 0.0 copy-start.9
  6.5 0.0 all-gather.4.cloned.1.call-start
  6.6 2.6 %convolution_convert_fusion.2 = bf16[512,512]{1,0:T(8,128)(2,1)} fusion(bf16[512,512]{1,0:T(8,128)(2,1)} %param.13, bf16[512,512]{1,0:T(8,128)(2,1)} %param.18), kind=kOutput, calls=%fused_computation.25 | convolution fusion | flops 268697600 | bytes 1572864 | tf_op jit(solution)/shard_map/dot_general | solution.py:62
  9.2 0.0 all-gather.4.cloned.1.call-update
  9.2 0.0 all-gather.6.cloned.1.call-start
  9.2 2.4 %convolution_convert_fusion.1 = bf16[512,512]{1,0:T(8,128)(2,1)} fusion(bf16[512,512]{1,0:T(8,128)(2,1)} %param.13, bf16[512,512]{1,0:T(8,128)(2,1)} %param.19), kind=kOutput, calls=%fused_computation.24 | convolution fusion | flops 268697600 | bytes 1572864 | tf_op jit(solution)/shard_map/dot_general | solution.py:63
  11.7 0.0 all-gather.6.cloned.1.call-update
  11.7 0.0 copy-done.4
  11.7 0.1 copy.22
  11.8 0.0 copy-done.1
  11.8 0.0 copy-done.9
  11.8 1.8 %fusion.11 = bf16[512,1024]{0,1:T(8,128)(2,1)S(1)} fusion(bf16[512,512]{1,0:T(8,128)(2,1)S(1)} %copy-done.1, bf16[512,512]{1,0:T(8,128)(2,1)S(1)} %copy-done.9, bf16[512,512]{1,0:T(8,128)(2,1)} %param.15), kind=kOutput, calls=%fused_computation.21 | convolution fusion | flops 539492352 | bytes 2621440 | tf_op jit(solution)/shard_map/dot_general | solution.py:34
  13.6 0.5 copy.23
  14.2 0.1 reshape_squeeze.10
  14.3 0.1 copy.21
  14.4 9.6 %gather_fusion.1 = bf16[2048,1024]{1,0:T(8,128)(2,1)} fusion(bf16[512,1024]{1,0:T(8,128)(2,1)S(1)} %copy.23, s32[2048]{0:T(1024)S(1)} %broadcast_clamp_fusion), kind=kCustom, calls=%fused_computation.1 | custom fusion | bytes 8396800 | tf_op jit(solution)/shard_map/jit(_take)/gather | solution.py:37
  24.0 4.1 %broadcast_select_fusion = bf16[64,32,1024]{2,1,0:T(8,128)(2,1)} fusion(bf16[64,32,1024]{2,1,0:T(8,128)(2,1)} %bitcast.46, pred[64,32]{1,0:T(8,128)(4,1)S(1)} %copy.21), kind=kLoop, calls=%fused_computation.16 | loop fusion | flops 2097152 | bytes 8390656 | tf_op jit(solution)/shard_map/jit(_take)/select_n | solution.py:37
  28.2 0.0 copy-start.5
  28.2 0.0 copy-start.8
  28.2 0.0 copy-start.3
  28.2 13.2 %all-to-all-start = ((bf16[64,32,1024]{2,1,0:T(8,128)(2,1)}), bf16[64,32,1024]{2,1,0:T(8,128)(2,1)}, u32[]{:S(2)}, u32[]{:S(2)}) async-start(bf16[64,32,1024]{2,1,0:T(8,128)(2,1)} %broadcast_select_fusion), calls=%async_computation | async-start | bytes 8388608 | tf_op jit(solution)/shard_map/all_to_all | solution.py:38
  41.3 0.0 copy-done.5
  41.3 0.1 copy.19
  41.4 0.1 eq.35
  41.5 0.1 reshape_squeeze.8
  41.6 0.0 copy-done.8
  41.6 0.1 iota_compare_fusion.2
  41.7 0.1 lt.67
  41.8 0.0 copy-done.3
  41.8 0.4 fusion.30
  42.2 0.0 copy-start.6
  42.3 0.0 copy-start.2
  42.3 8.9 %gather_fusion = f32[2048,512]{1,0:T(8,128)} fusion(f32[512,512]{1,0:T(8,128)S(1)} %fusion.30, s32[2048]{0:T(1024)S(1)} %broadcast_clamp_fusion.1), kind=kCustom, calls=%fused_computation | custom fusion | bytes 8396800 | tf_op jit(solution)/shard_map/jit(_take)/gather | solution.py:45
  51.2 0.0 copy-done.6
  51.2 9.8 %all-gather = s32[1,2048]{1,0:T(1,128)S(1)} all-gather(s32[1,512]{1,0:T(1,128)S(1)} %copy-done.6), channel_id=2, replica_groups=mesh['dom'=64,'loop'=4] {'loop'}, dimensions={1}, use_global_device_ids=true | all-gather | bytes 10240 | tf_op jit(solution)/shard_map/all_gather | solution.py:76
  61.0 0.0 copy-done.2
  61.0 0.5 convolution_convert_fusion.3
  61.5 0.7 broadcast_compare_fusion
  62.1 0.0 all-gather.4.cloned.1.call-done
  62.1 3.9 %copy.24 = bf16[2048,512]{0,1:T(8,128)(2,1)} copy(bf16[2048,512]{1,0:T(8,128)(2,1)} %all-gather.4.cloned.1.call-done) | data formatting | bytes 4194304 | tf_op jit(solution)/shard_map/all_gather | solution.py:68
  66.1 15.8 %all-gather.6.cloned.1.call-done = bf16[2048,512]{1,0:T(8,128)(2,1)} async-done(((bf16[512,512]{1,0:T(8,128)(2,1)}), bf16[2048,512]{1,0:T(8,128)(2,1)}) %all-gather.6.cloned.1.call-update) | async-done | bytes 2097168 | tf_op jit(solution)/shard_map/all_gather | solution.py:69
  81.9 4.0 %copy.25 = bf16[2048,512]{0,1:T(8,128)(2,1)} copy(bf16[2048,512]{1,0:T(8,128)(2,1)} %all-gather.6.cloned.1.call-done) | data formatting | bytes 4194304 | tf_op jit(solution)/shard_map/all_gather | solution.py:69
  85.8 15.4 %fusion = (f32[8,512]{1,0:T(8,128)S(1)}, f32[8,512,2048]{2,1,0:T(8,128)}) fusion(pred[512,2048]{1,0:T(8,128)(4,1)S(1)} %broadcast_compare_fusion, bf16[512,8,64]{0,2,1:T(8,128)(2,1)S(1)} %bitcast.48, bf16[2048,8,64]{0,2,1:T(8,128)(2,1)} %bitcast.47), kind=kOutput, calls=%fused_computation.4 | convolution fusion | flops 1098903552 | bytes 37240832 | tf_op jit(solution)/shard_map/qhd,khd->hqk/dot_general | solution.py:73
  101.2 15.5 %fusion.1 = f32[8,512]{1,0:T(8,128)S(1)} fusion(f32[8,512,2048]{2,1,0:T(8,128)} %get-tuple-element.10, f32[8,512]{1,0:T(8,128)S(1)} %get-tuple-element.8, pred[512,2048]{1,0:T(8,128)(4,1)S(1)} %broadcast_compare_fusion), kind=kLoop, calls=%fused_computation.5 | loop fusion | flops 41938944 | bytes 34635776 | tf_op jit(solution)/shard_map/reduce_sum | solution.py:81
  116.8 15.3 %divide_convert_fusion = bf16[512,8,64]{0,2,1:T(8,128)(2,1)S(1)} fusion(bf16[2048,8,64]{0,2,1:T(8,128)(2,1)} %bitcast.49, f32[8,512,2048]{2,1,0:T(8,128)} %get-tuple-element.10, f32[8,512]{1,0:T(8,128)S(1)} %get-tuple-element.8, pred[512,2048]{1,0:T(8,128)(4,1)S(1)} %broadcast_compare_fusion, f32[512,8]{0,1:T(8,128)S(1)} %bitcast.53, ...), kind=kOutput, calls=%fused_computation.35 | convolution fusion | flops 1116471296 | bytes 37273600 | tf_op jit(solution)/shard_map/hqk,khd->qhd/dot_general | solution.py:82
  132.1 5.2 %all-to-all-done = bf16[64,32,1024]{2,1,0:T(8,128)(2,1)} async-done(((bf16[64,32,1024]{2,1,0:T(8,128)(2,1)}), bf16[64,32,1024]{2,1,0:T(8,128)(2,1)}, u32[]{:S(2)}, u32[]{:S(2)}) %all-to-all-start) | async-done | bytes 4194336 | tf_op jit(solution)/shard_map/all_to_all | solution.py:38
  137.2 5.4 %convert_multiply_fusion = (f32[2048,512]{1,0:T(8,128)S(1)}, f32[2048,512]{1,0:T(8,128)S(1)}) fusion(bf16[2048,1024]{1,0:T(8,128)(2,1)} %bitcast.6, f32[2048,512]{1,0:T(8,128)} %gather_fusion, pred[2048]{0:T(1024)(128)(4,1)S(1)} %compare_and_fusion.1, pred[2048]{0:T(1024)(128)(4,1)S(1)} %lt.67), kind=kLoop, calls=%fused_computation.13 | loop fusion | flops 9437184 | bytes 16781312 | tf_op jit(solution)/shard_map/mul | solution.py:50
  142.6 7.2 %fusion.6 = f32[512,1024]{1,0:T(8,128)S(1)} fusion(f32[2048,512]{1,0:T(8,128)S(1)} %get-tuple-element.6, f32[2048,512]{1,0:T(8,128)S(1)} %get-tuple-element.5, s32[2048]{0:T(1024)S(1)} %eq.35), kind=kOutput, calls=%fused_computation.9 | convolution fusion | flops 12888047616 | bytes 10493952 | tf_op jit(solution)/shard_map/dot_general | solution.py:51
  149.8 0.0 copy-start.7
  149.8 0.0 copy-done
  149.9 0.6 multiply_reduce_fusion
  150.5 0.0 copy-done.7
  150.5 1.0 multiply_convert_fusion
  (8 shorter events, 0.1 us)
Async XLA Ops:
  6.5 143.3 %copy-start = (bf16[512,512]{1,0:T(8,128)(2,1)S(1)}, bf16[512,512]{1,0:T(8,128)(2,1)}, u32[]{:S(2)}) copy-start(bf16[512,512]{1,0:T(8,128)(2,1)} %param.20) | copy-start | bytes 1572868
  6.5 5.3 %copy-start.1 = (bf16[512,512]{1,0:T(8,128)(2,1)S(1)}, bf16[512,512]{1,0:T(8,128)(2,1)}, u32[]{:S(2)}) copy-start(bf16[512,512]{1,0:T(8,128)(2,1)} %param.13) | copy-start | bytes 1572868
  6.5 5.2 %copy-start.4 = (s32[1,1,64,32]{2,3,1,0:T(8,128)S(1)}, s32[1,1,64,32]{2,3,1,0:T(8,128)}, u32[]{:S(2)}) copy-start(s32[1,1,64,32]{2,3,1,0:T(8,128)} %param.22) | copy-start | bytes 24580
  6.5 5.3 %copy-start.9 = (bf16[512,512]{1,0:T(8,128)(2,1)S(1)}, bf16[512,512]{1,0:T(8,128)(2,1)}, u32[]{:S(2)}) copy-start(bf16[512,512]{1,0:T(8,128)(2,1)} %param.16) | copy-start | bytes 1572868
  6.5 55.6 %all-gather.4.cloned.1.call-start = ((), (), s32[]{:S(2)}) async-start(), calls=%async_computation.1 | async-start | bytes 2621440 | tf_op jit(solution)/shard_map/all_gather | solution.py:68
  9.2 72.7 %all-gather.6.cloned.1.call-start = ((), (), s32[]{:S(2)}) async-start(), calls=%async_computation.2 | async-start | bytes 2621440 | tf_op jit(solution)/shard_map/all_gather | solution.py:69
  28.2 13.2 %copy-start.5 = (s32[1,1,64,32]{2,3,1,0:T(8,128)S(1)}, s32[1,1,64,32]{2,3,1,0:T(8,128)}, u32[]{:S(2)}) copy-start(s32[1,1,64,32]{2,3,1,0:T(8,128)} %param.23) | copy-start | bytes 24580
  28.2 13.4 %copy-start.8 = (s32[1,1,64]{2,1,0:T(1,128)S(1)}, s32[1,1,64]{2,1,0:T(1,128)}, u32[]{:S(2)}) copy-start(s32[1,1,64]{2,1,0:T(1,128)} %param.24) | copy-start | bytes 772
  28.2 13.6 %copy-start.3 = (bf16[512,512]{1,0:T(8,128)(2,1)S(1)}, bf16[512,512]{1,0:T(8,128)(2,1)}, u32[]{:S(2)}) copy-start(bf16[512,512]{1,0:T(8,128)(2,1)} %param.14) | copy-start | bytes 1572868
  28.2 109.0 %all-to-all-start = ((bf16[64,32,1024]{2,1,0:T(8,128)(2,1)}), bf16[64,32,1024]{2,1,0:T(8,128)(2,1)}, u32[]{:S(2)}, u32[]{:S(2)}) async-start(bf16[64,32,1024]{2,1,0:T(8,128)(2,1)} %broadcast_select_fusion), calls=%async_computation | async-start | bytes 8388608 | tf_op jit(solution)/shard_map/all_to_all | solution.py:38
  42.2 8.9 %copy-start.6 = (s32[1,512]{1,0:T(1,128)S(1)}, s32[1,512]{1,0:T(1,128)}, u32[]{:S(2)}) copy-start(s32[1,512]{1,0:T(1,128)} %param.25) | copy-start | bytes 6148
  42.3 18.7 %copy-start.2 = (bf16[512,512]{1,0:T(8,128)(2,1)S(1)}, bf16[512,512]{1,0:T(8,128)(2,1)}, u32[]{:S(2)}) copy-start(bf16[512,512]{1,0:T(8,128)(2,1)} %param.17) | copy-start | bytes 1572868
  149.8 0.7 copy-start.7
Sparse Core Ops, SparseCore 0:
  9.3 37.2 all-gather.3
  48.4 33.4 all-gather.5
where the time goes:
time: 159 us; the launch traced here: 158 us
  matrix products  46.2 us (29%)
  local copies, waits for them, and re-layouts  27.7 us (17%)
  other arithmetic  26.8 us (17%)
  waiting for transfers between devices  21 us (13%)
  between operations  13.6 us (9%)
  starting transfers between devices  13.2 us (8%)
  blocking collectives  9.77 us (6%)
    all_gather x1, waiting for transfers between devices, per_device(): lax.all_gather(value_rows, 'loop', axis=0, tiled=True)  15.8 us
    reduce_sum x1, other arithmetic, per_device(): weight_sum = jnp.sum(weights, axis=-1)  15.5 us
    dot_general x1, matrix products, per_device(): jnp.einsum('qhd,khd->hqk', queries, key_heads, preferred_element_type=jnp...  15.4 us
    dot_general x1, matrix products, per_device(): jnp.einsum('hqk,khd->qhd', weights.astype(jnp.bfloat16), value_heads, pre...  15.3 us
    all_to_all x1, starting transfers between devices, per_device(): lax.all_to_all(outgoing, 'dom', split_axis=0, concat_axis=0, tiled=True)  13.2 us
    all_gather x1, blocking collectives, per_device(): lax.all_gather(own_ids, 'loop', axis=0, tiled=True)[None, :]  9.77 us
    gather x1, local copies, waits for them, and re-layouts, per_device(): jnp.take(projected, selected, axis=0).reshape(peers, slots, 2 * D)  9.63 us
    gather x1, local copies, waits for them, and re-layouts, per_device(): jnp.take(dst_term, targets, axis=0) + edge_src.astype(jnp.float32)  8.9 us
  transfers between devices with their start and end apart: 3, of which 2 were waited for; matrix products, arithmetic and copies ran while one was open for 53% of the time, Pallas kernels for 0%

commit v1 on v0

v1 whole, which is shorter than its diff:
```python
import math

import jax
import jax.numpy as jnp
from jax import lax
from jax.experimental import pallas as pl
from jax.experimental.pallas import tpu as pltpu
from jax.sharding import PartitionSpec as P

MESH = pl.DeviceIdType.MESH
BF16 = jnp.bfloat16
F32 = jnp.float32
D = 512
ROWS = 512
HEADS = 8
PAIRS = 4
HEAD_DIM = 64
CAP = 32
LOOPS = 4
NX, NZ, NC = 4, 8, 2
GROUP = NX * NC
SLOTS = GROUP * CAP
KEYS = LOOPS * ROWS
QB = 256
BIG = 1e30
ORDER = (4, 3, 5, 2, 6, 1, 7, 0)


def dot(a, b):
    return jnp.dot(a, b, preferred_element_type=F32)


def dot_t(a, b):
    return lax.dot_general(a, b, (((0,), (0,)), ((), ())), preferred_element_type=F32)


def dot_nt(a, b):
    return lax.dot_general(a, b, (((1,), (1,)), ((), ())), preferred_element_type=F32)


def kernel(
    rows_hbm,
    wdst_hbm,
    wsrc_hbm,
    wval_hbm,
    wq_hbm,
    wk_hbm,
    wv_hbm,
    wout_hbm,
    gain_ref,
    send_ref,
    dstrow_ref,
    counts_ref,
    ids_ref,
    out_ref,
    rows,
    ids,
    wdst,
    wsv,
    wq,
    wk,
    wv,
    wout,
    outgoing,
    incoming,
    dsthl,
    kx,
    vx,
    qp,
    qmask,
    mixed,
    base,
    acc,
    in_sem,
    y_send,
    y_recv,
    i_send,
    i_recv,
    e_send,
    e_recv,
):
    dom = lax.axis_index("dom")
    lp = lax.axis_index("loop")
    x, z, c = dom // (NZ * NC), (dom // NC) % NZ, dom % NC

    def peer(j, i, sign):
        dx, dc = i // NC, i % NC
        px = (x + sign * dx + NX) % NX
        pz = (z + sign * j + NZ) % NZ
        pc = (c + dc) % NC
        return (px * NZ + pz) * NC + pc

    loads = [
        pltpu.make_async_copy(src, dst, in_sem.at[n])
        for n, (src, dst) in enumerate(
            [
                (rows_hbm, rows.at[0]),
                (wdst_hbm, wdst),
                (wq_hbm, wq),
                (wk_hbm, wk),
                (wv_hbm, wv),
                (wsrc_hbm, wsv.at[:, pl.ds(0, D)]),
                (wval_hbm, wsv.at[:, pl.ds(D, D)]),
                (wout_hbm, wout),
            ]
        )
    ]
    for cp in loads:
        cp.start()

    barrier = pltpu.get_barrier_semaphore()
    for k in range(1, LOOPS):
        pl.semaphore_signal(barrier, inc=1, device_id=(dom, (lp + k) % LOOPS), device_id_type=MESH)
    for j in ORDER:
        for i in range(GROUP):
            if (j, i) != (0, 0):
                pl.semaphore_signal(barrier, inc=1, device_id=(peer(j, i, 1), lp), device_id_type=MESH)

    ids[0] = ids_ref[...]
    loads[0].wait()
    row_of = lax.broadcasted_iota(jnp.int32, (ROWS, SLOTS), 0)

    copies = []
    for n, j in enumerate(ORDER):
        picks = jnp.concatenate([send_ref[pl.ds(peer(j, i, 1), 1), :] for i in range(GROUP)], axis=1)
        onehot = (row_of == picks).astype(BF16)
        picked = dot_t(onehot, rows[0]).astype(BF16)
        if j == 0:
            incoming[0, pl.ds(0, CAP), :] = picked[:CAP]
        outgoing[j] = picked
        if n == 0:
            pl.semaphore_wait(barrier, LOOPS - 1 + NX * NZ * NC - 1)
            for k in (2, 1, 3):
                to = (dom, (lp + k) % LOOPS)
                for src, dst, ss, rs in (
                    (ids.at[0], ids.at[k], i_send, i_recv),
                    (rows.at[0], rows.at[k], y_send, y_recv),
                ):
                    cp = pltpu.make_async_remote_copy(
                        src_ref=src,
                        dst_ref=dst,
                        send_sem=ss.at[k],
                        recv_sem=rs.at[k],
                        device_id=to,
                        device_id_type=MESH,
                    )
                    cp.start()
                    copies.append(cp)
        for i in range(GROUP):
            if (j, i) == (0, 0):
                continue
            cp = pltpu.make_async_remote_copy(
                src_ref=outgoing.at[j, pl.ds(i * CAP, CAP)],
                dst_ref=incoming.at[j, pl.ds(i * CAP, CAP)],
                send_sem=e_send.at[j, i],
                recv_sem=e_recv.at[j, i],
                device_id=(peer(j, i, 1), lp),
                device_id_type=MESH,
            )
            cp.start()
            copies.append(cp)
    y_copies = copies[:6]
    e_copies = copies[6:]

    loads[1].wait()
    dst_term = dot(rows[0], wdst[...])
    high = dst_term.astype(BF16)
    dsthl[:, :D] = high
    dsthl[:, D:] = (dst_term - high.astype(F32)).astype(BF16)
    loads[2].wait()
    q_all = dot(rows[0], wq[...]).astype(BF16)
    for pair in range(PAIRS):
        qp[pair] = q_all[:, pair * 128 : (pair + 1) * 128]
    loads[3].wait()
    loads[4].wait()

    def column_ids(k, b):
        line = ids[k, :, pl.ds(b * 128, 128)]
        return jnp.transpose(jnp.broadcast_to(line, (128, 128)))

    lane = lax.broadcasted_iota(jnp.int32, (128, 128), 1)
    for b in range(ROWS // 128):
        own = column_ids(0, b)
        qmask[pl.ds(b * 128, 128), :] = jnp.where((lane == own) | (lane >= 2), 0.0, -BIG).astype(BF16)

    for k in range(LOOPS):
        if k:
            for cp in y_copies:
                pass
            n = {2: 0, 1: 1, 3: 2}[k]
            y_copies[2 * n].wait_recv()
            y_copies[2 * n + 1].wait_recv()
        slab = rows[k]
        keys = dot(slab, wk[...]).astype(BF16)
        values = dot(slab, wv[...]).astype(BF16)
        for pair in range(PAIRS):
            kx[pair, pl.ds(k * ROWS, ROWS), :128] = keys[:, pair * 128 : (pair + 1) * 128]
            vx[pair, pl.ds(k * ROWS, ROWS), :128] = values[:, pair * 128 : (pair + 1) * 128]
            vx[pair, pl.ds(k * ROWS, ROWS), 128:] = jnp.ones((ROWS, 128), BF16)
        for b in range(ROWS // 128):
            hit = jnp.where(lane == column_ids(k, b), 1.0, 0.0).astype(BF16)
            for pair in range(PAIRS):
                kx[pair, pl.ds(k * ROWS + b * 128, 128), 128:] = hit

    half = lax.broadcasted_iota(jnp.int32, (QB, 128), 1) < HEAD_DIM
    exponent = math.log2(math.e) / math.sqrt(HEAD_DIM)

    def attend(step, carry):
        pair, block = step // (ROWS // QB), step % (ROWS // QB)
        at = pl.ds(pl.multiple_of(block * QB, QB), QB)
        queries = qp[pair, at, :]
        mask = qmask[at, :]
        sides = []
        for keep in (half, jnp.logical_not(half)):
            query = jnp.concatenate([jnp.where(keep, queries, 0).astype(BF16), mask], axis=1)
            scores = dot_nt(query, kx[pair])
            top = jnp.max(scores, axis=1, keepdims=True)
            weights = jnp.exp2((scores - top) * exponent).astype(BF16)
            sums = dot(weights, vx[pair])
            sides.append(sums[:, :128] / sums[:, 128:])
        mixed[pair, at, :] = jnp.where(half, sides[0], sides[1]).astype(BF16)
        return carry

    lax.fori_loop(0, PAIRS * (ROWS // QB), attend, 0)

    loads[7].wait()
    attended = rows[0].astype(F32)
    for pair in range(PAIRS):
        attended += dot(mixed[pair], wout[pl.ds(pair * 128, 128), :])
    base[...] = attended

    loads[5].wait()
    loads[6].wait()
    slot = lax.broadcasted_iota(jnp.int32, (1, CAP), 1)
    at = 0
    for n, j in enumerate(ORDER):
        for i in range(GROUP):
            if (j, i) != (0, 0):
                e_copies[at].wait_recv()
                at += 1
        lines = []
        for i in range(GROUP):
            q = peer(j, i, -1)
            lines.append(jnp.where(slot < counts_ref[0, q], dstrow_ref[pl.ds(q, 1), :], -1))
        targets = jnp.concatenate(lines, axis=1)
        onehot = (row_of == targets).astype(BF16)
        projected = dot(incoming[j], wsv[...]).astype(BF16).astype(F32)
        parts = dot_t(onehot, dsthl[...])
        gates = 0.5 + 0.5 * jnp.tanh(0.5 * (parts[:, :D] + parts[:, D:] + projected[:, :D]))
        stacked = jnp.concatenate([gates * projected[:, D:], gates], axis=1).astype(BF16)
        sums = dot(onehot, stacked)
        if n == 0:
            acc[...] = sums
        else:
            acc[...] += sums

    total = base[...] + acc[:, :D] / (1.0 + acc[:, D:])
    spread = lax.rsqrt(jnp.mean(total * total, axis=1, keepdims=True) + 1e-6)
    out_ref[...] = (total * spread * gain_ref[...]).astype(BF16)

    for cp in copies:
        cp.wait_send()


def per_device(
    node_rows,
    w_dst,
    w_src,
    w_val,
    w_query,
    w_key,
    w_value,
    w_out,
    norm_gain,
    send_rows,
    dst_rows,
    counts,
    batch_ids,
):
    hbm = pl.BlockSpec(memory_space=pl.ANY)
    vmem = pl.BlockSpec(memory_space=pltpu.VMEM)
    smem = pl.BlockSpec(memory_space=pltpu.SMEM)
    dma = pltpu.SemaphoreType.DMA
    return pl.pallas_call(
        kernel,
        out_shape=jax.ShapeDtypeStruct((ROWS, D), BF16),
        in_specs=[hbm] * 8 + [vmem] * 3 + [smem, vmem],
        out_specs=vmem,
        scratch_shapes=[
            pltpu.VMEM((LOOPS, ROWS, D), BF16),
            pltpu.VMEM((LOOPS, 1, ROWS), jnp.int32),
            pltpu.VMEM((D, D), BF16),
            pltpu.VMEM((D, 2 * D), BF16),
            pltpu.VMEM((D, D), BF16),
            pltpu.VMEM((D, D), BF16),
            pltpu.VMEM((D, D), BF16),
            pltpu.VMEM((D, D), BF16),
            pltpu.VMEM((NZ, SLOTS, D), BF16),
            pltpu.VMEM((NZ, SLOTS, D), BF16),
            pltpu.VMEM((ROWS, 2 * D), BF16),
            pltpu.VMEM((PAIRS, KEYS, 256), BF16),
            pltpu.VMEM((PAIRS, KEYS, 256), BF16),
            pltpu.VMEM((PAIRS, ROWS, 128), BF16),
            pltpu.VMEM((ROWS, 128), BF16),
            pltpu.VMEM((PAIRS, ROWS, 128), BF16),
            pltpu.VMEM((ROWS, D), F32),
            pltpu.VMEM((ROWS, 2 * D), F32),
            dma((8,)),
            dma((LOOPS,)),
            dma((LOOPS,)),
            dma((LOOPS,)),
            dma((LOOPS,)),
            dma((NZ, GROUP)),
            dma((NZ, GROUP)),
        ],
        compiler_params=pltpu.CompilerParams(
            collective_id=0, has_side_effects=True, vmem_limit_bytes=56 * 2**20
        ),
        cost_estimate=pl.CostEstimate(flops=14 * 10**9, bytes_accessed=5 * 2**20, transcendentals=9 * 10**6),
    )(
        node_rows,
        w_dst,
        w_src,
        w_val,
        w_query,
        w_key,
        w_value,
        w_out,
        norm_gain.reshape(1, D),
        send_rows.reshape(send_rows.shape[2:]),
        dst_rows.reshape(dst_rows.shape[2:]),
        counts.reshape(1, -1),
        batch_ids,
    )


def solution(mesh):
    return jax.shard_map(
        per_device,
        mesh=mesh,
        in_specs=(
            P(("dom", "loop"), None),
            P(),
            P(),
            P(),
            P(),
            P(),
            P(),
            P(),
            P(),
            P("dom", "loop", None, None),
            P("dom", "loop", None, None),
            P("dom", "loop", None),
            P("dom", "loop"),
        ),
        out_specs=P(("dom", "loop"), None),
        check_vma=False,
    )
```

time: 159 us -> 75 us (0.47)
  Pallas kernels: 0 us -> 70.8 us
  matrix products: 46.2 us -> 0 us
  other arithmetic: 26.8 us -> 0 us
  local copies, waits for them, and re-layouts: 27.7 us -> 3.99 us
  waiting for transfers between devices: 21 us -> 0 us
  between operations: 13.6 us -> 0.01 us
  starting transfers between devices: 13.2 us -> 0 us
  blocking collectives: 9.77 us -> 0 us
    pallas_call x0 -> x1, Pallas kernels: none -> 70.8 us  [per_device(): pl.pallas_call(kernel, out_shape=jax.ShapeDtypeStruct((ROWS, D), BF16), i...]
    dot_general x9 -> x0, matrix products: 46.2 us -> none  [the longest x1 15.4 us: per_device(): jnp.einsum('qhd,khd->hqk', queries, key_heads, preferred_element_type=jnp...]
    gather x2 -> x0, local copies, waits for them, and re-layouts: 18.5 us -> none  [the longest x1 9.63 us: per_device(): jnp.take(projected, selected, axis=0).reshape(peers, slots, 2 * D)]
    all_gather x2 -> x0, waiting for transfers between devices: 15.8 us -> none  [the longest x1 15.8 us: per_device(): lax.all_gather(value_rows, 'loop', axis=0, tiled=True)]
    reduce_sum x1 -> x0, other arithmetic: 15.5 us -> none  [per_device(): weight_sum = jnp.sum(weights, axis=-1)]
    all_to_all x1 -> x0, starting transfers between devices: 13.2 us -> none  [per_device(): lax.all_to_all(outgoing, 'dom', split_axis=0, concat_axis=0, tiled=True)]
    all_gather x1 -> x0, blocking collectives: 9.77 us -> none  [per_device(): lax.all_gather(own_ids, 'loop', axis=0, tiled=True)[None, :]]
    all_gather x2 -> x0, local copies, waits for them, and re-layouts: 7.94 us -> none  [the longest x1 4 us: per_device(): lax.all_gather(value_rows, 'loop', axis=0, tiled=True)]
  transfers between devices with their start and end apart: 3 -> 0, of which waited for: 2 -> 0; matrix products, arithmetic and copies ran while one was open for 53% -> 0% of each run, Pallas kernels for 0% -> 0%
where the time goes in v1:
time: 75 us; the launch traced here: 74.8 us
  Pallas kernels  70.8 us (94%)
  local copies, waits for them, and re-layouts  3.99 us (5%)
    pallas_call x1, Pallas kernels, per_device(): pl.pallas_call(kernel, out_shape=jax.ShapeDtypeStruct((ROWS, D), BF16), i...  70.8 us
    unnamed x5, local copies, waits for them, and re-layouts  3.99 us

profile of v1, /device:TPU:1, one launch (start us, length us, event | category | flops | bytes accessed | tf_op | source)
XLA Modules:
  0.0 74.8 jit_solution(5714780840245241574)
XLA Ops:
  0.0 0.0 copy-start
  0.0 1.4 %copy.14 = s32[1,1,64,32]{3,2,1,0:T(8,128)} copy(s32[1,1,64,32]{2,3,1,0:T(8,128)} %param.22) | data formatting | bytes 16384 | tf_op args[9]
  1.4 0.0 copy-done
  1.4 0.7 copy.15
  2.1 70.8 %shard_map.127 = bf16[512,512]{1,0:T(8,128)(2,1)} custom-call(bf16[512,512]{1,0:T(8,128)(2,1)} %rows_hbm.1, bf16[512,512]{1,0:T(8,128)(2,1)} %wdst_hbm.1, bf16[512,512]{1,0:T(8,128)(2,1)} %wsrc_hbm.1, bf16[512,512]{1,0:T(8,128)(2,1)} %wval_hbm.1, bf16[512,512]{1,0:T(8,128)(2,1)} %wq_hbm.1, bf16[512,512]{1,0:T(8,128)(2,1)} %wk_hbm.1, ...), custom_call_target="tpu_custom_call" | custom-call | flops 14000000000 | bytes 5242880 | tf_op jit(solution)/shard_map/pallas_call | solution.py:284
  72.9 1.9 %copy.17 = bf16[512,512]{1,0:T(8,128)(2,1)} copy(bf16[512,512]{1,0:T(8,128)(2,1)} %shard_map.127) | data formatting | bytes 1048576
Async XLA Ops:
  0.0 1.4 %copy-start = (s32[1,1,64,32]{2,3,1,0:T(8,128)S(1)}, s32[1,1,64,32]{2,3,1,0:T(8,128)}, u32[]{:S(2)}) copy-start(s32[1,1,64,32]{2,3,1,0:T(8,128)} %param.23) | copy-start | bytes 24580

commit v2 on v1

--- a/solution.py
+++ b/solution.py
@@ -19,11 +19,12 @@
 LOOPS = 4
 NX, NZ, NC = 4, 8, 2
 GROUP = NX * NC
+PEERS = NX * NZ * NC
 SLOTS = GROUP * CAP
 KEYS = LOOPS * ROWS
-QB = 256
 BIG = 1e30
 ORDER = (4, 3, 5, 2, 6, 1, 7, 0)
+LATER = (1, 3, 2)
 
 
 def dot(a, b):
@@ -47,14 +48,18 @@
     wk_hbm,
     wv_hbm,
     wout_hbm,
-    gain_ref,
-    send_ref,
-    dstrow_ref,
-    counts_ref,
-    ids_ref,
+    send_hbm,
+    dstrow_hbm,
+    counts_hbm,
+    ids_hbm,
     out_ref,
     rows,
     ids,
+    send_in,
+    dstrow_in,
+    counts_ref,
+    send_ref,
+    dstrow_ref,
     wdst,
     wsv,
     wq,
@@ -64,6 +69,8 @@
     outgoing,
     incoming,
     dsthl,
+    hits,
+    received,
     kx,
     vx,
     qp,
@@ -95,6 +102,10 @@
         for n, (src, dst) in enumerate(
             [
                 (rows_hbm, rows.at[0]),
+                (send_hbm, send_in),
+                (ids_hbm, ids.at[0]),
+                (dstrow_hbm, dstrow_in),
+                (counts_hbm, counts_ref),
                 (wdst_hbm, wdst),
                 (wq_hbm, wq),
                 (wk_hbm, wk),
@@ -105,7 +116,7 @@
             ]
         )
     ]
-    for cp in loads:
+    for cp in loads[:3]:
         cp.start()
 
     barrier = pltpu.get_barrier_semaphore()
@@ -116,13 +127,22 @@
             if (j, i) != (0, 0):
                 pl.semaphore_signal(barrier, inc=1, device_id=(peer(j, i, 1), lp), device_id_type=MESH)
 
-    ids[0] = ids_ref[...]
+    for cp in loads[3:]:
+        cp.start()
+
+    def by_peer(block):
+        wide = jnp.concatenate([block, jnp.zeros((CAP, 128 - block.shape[1]), jnp.int32)], axis=1)
+        return jnp.transpose(jnp.concatenate([wide, jnp.zeros((128 - CAP, 128), jnp.int32)], axis=0))
+
+    loads[1].wait()
+    send_ref[...] = by_peer(send_in[...])
     loads[0].wait()
+    loads[2].wait()
     row_of = lax.broadcasted_iota(jnp.int32, (ROWS, SLOTS), 0)
 
     copies = []
     for n, j in enumerate(ORDER):
-        picks = jnp.concatenate([send_ref[pl.ds(peer(j, i, 1), 1), :] for i in range(GROUP)], axis=1)
+        picks = jnp.concatenate([send_ref[pl.ds(peer(j, i, 1), 1), :CAP] for i in range(GROUP)], axis=1)
         onehot = (row_of == picks).astype(BF16)
         picked = dot_t(onehot, rows[0]).astype(BF16)
         if j == 0:
@@ -130,7 +150,7 @@
         outgoing[j] = picked
         if n == 0:
             pl.semaphore_wait(barrier, LOOPS - 1 + NX * NZ * NC - 1)
-            for k in (2, 1, 3):
+            for k in LATER:
                 to = (dom, (lp + k) % LOOPS)
                 for src, dst, ss, rs in (
                     (ids.at[0], ids.at[k], i_send, i_recv),
@@ -162,17 +182,17 @@
     y_copies = copies[:6]
     e_copies = copies[6:]
 
-    loads[1].wait()
+    loads[5].wait()
     dst_term = dot(rows[0], wdst[...])
     high = dst_term.astype(BF16)
     dsthl[:, :D] = high
     dsthl[:, D:] = (dst_term - high.astype(F32)).astype(BF16)
-    loads[2].wait()
+    loads[6].wait()
     q_all = dot(rows[0], wq[...]).astype(BF16)
     for pair in range(PAIRS):
         qp[pair] = q_all[:, pair * 128 : (pair + 1) * 128]
-    loads[3].wait()
-    loads[4].wait()
+    loads[7].wait()
+    loads[8].wait()
 
     def column_ids(k, b):
         line = ids[k, :, pl.ds(b * 128, 128)]
@@ -183,80 +203,84 @@
         own = column_ids(0, b)
         qmask[pl.ds(b * 128, 128), :] = jnp.where((lane == own) | (lane >= 2), 0.0, -BIG).astype(BF16)
 
-    for k in range(LOOPS):
-        if k:
-            for cp in y_copies:
-                pass
-            n = {2: 0, 1: 1, 3: 2}[k]
-            y_copies[2 * n].wait_recv()
-            y_copies[2 * n + 1].wait_recv()
+    half = lax.broadcasted_iota(jnp.int32, (ROWS, 128), 1) < HEAD_DIM
+    exponent = math.log2(math.e) / math.sqrt(HEAD_DIM)
+
+    def project(k, place):
+        to = pl.ds(place * ROWS, ROWS)
         slab = rows[k]
+        hit = jnp.where(lax.broadcasted_iota(jnp.int32, (128, ROWS), 0) == ids[k], 1.0, 0.0).astype(BF16)
         keys = dot(slab, wk[...]).astype(BF16)
         values = dot(slab, wv[...]).astype(BF16)
         for pair in range(PAIRS):
-            kx[pair, pl.ds(k * ROWS, ROWS), :128] = keys[:, pair * 128 : (pair + 1) * 128]
-            vx[pair, pl.ds(k * ROWS, ROWS), :128] = values[:, pair * 128 : (pair + 1) * 128]
-            vx[pair, pl.ds(k * ROWS, ROWS), 128:] = jnp.ones((ROWS, 128), BF16)
-        for b in range(ROWS // 128):
-            hit = jnp.where(lane == column_ids(k, b), 1.0, 0.0).astype(BF16)
-            for pair in range(PAIRS):
-                kx[pair, pl.ds(k * ROWS + b * 128, 128), 128:] = hit
-
-    half = lax.broadcasted_iota(jnp.int32, (QB, 128), 1) < HEAD_DIM
-    exponent = math.log2(math.e) / math.sqrt(HEAD_DIM)
-
-    def attend(step, carry):
-        pair, block = step // (ROWS // QB), step % (ROWS // QB)
-        at = pl.ds(pl.multiple_of(block * QB, QB), QB)
-        queries = qp[pair, at, :]
-        mask = qmask[at, :]
+            kx[pair, :128, to] = jnp.transpose(keys[:, pair * 128 : (pair + 1) * 128])
+            kx[pair, 128:, to] = hit
+            vx[pair, to, :128] = values[:, pair * 128 : (pair + 1) * 128]
+            vx[pair, to, 128:] = jnp.ones((ROWS, 128), BF16)
+
+    loads[3].wait()
+    loads[4].wait()
+    dstrow_ref[...] = by_peer(dstrow_in[...])
+    slot = lax.broadcasted_iota(jnp.int32, (1, CAP), 1)
+
+    def targets_of(j, carry):
+        lines = []
+        for i in range(GROUP):
+            q = peer(j, i, -1)
+            lines.append(jnp.where(slot < counts_ref[0, q], dstrow_ref[pl.ds(q, 1), :CAP], -1))
+        onehot = (row_of == jnp.concatenate(lines, axis=1)).astype(BF16)
+        hits[j] = onehot
+        parts = dot_t(onehot, dsthl[...])
+        received[j] = parts[:, :D] + parts[:, D:]
+        return carry
+
+    lax.fori_loop(0, NZ, targets_of, 0)
+    project(0, 0)
+    for n, k in enumerate(LATER):
+        y_copies[2 * n].wait_recv()
+        y_copies[2 * n + 1].wait_recv()
+        project(k, n + 1)
+
+    def attend(pair, carry):
+        queries = qp[pair]
         sides = []
         for keep in (half, jnp.logical_not(half)):
-            query = jnp.concatenate([jnp.where(keep, queries, 0).astype(BF16), mask], axis=1)
-            scores = dot_nt(query, kx[pair])
+            query = jnp.concatenate([jnp.where(keep, queries, 0).astype(BF16), qmask[...]], axis=1)
+            scores = dot(query, kx[pair])
             top = jnp.max(scores, axis=1, keepdims=True)
             weights = jnp.exp2((scores - top) * exponent).astype(BF16)
             sums = dot(weights, vx[pair])
             sides.append(sums[:, :128] / sums[:, 128:])
-        mixed[pair, at, :] = jnp.where(half, sides[0], sides[1]).astype(BF16)
+        mixed[pair] = jnp.where(half, sides[0], sides[1]).astype(BF16)
         return carry
 
-    lax.fori_loop(0, PAIRS * (ROWS // QB), attend, 0)
-
-    loads[7].wait()
+    lax.fori_loop(0, PAIRS, attend, 0)
+
+    loads[11].wait()
     attended = rows[0].astype(F32)
     for pair in range(PAIRS):
         attended += dot(mixed[pair], wout[pl.ds(pair * 128, 128), :])
     base[...] = attended
 
-    loads[5].wait()
-    loads[6].wait()
-    slot = lax.broadcasted_iota(jnp.int32, (1, CAP), 1)
+    loads[9].wait()
+    loads[10].wait()
     at = 0
     for n, j in enumerate(ORDER):
         for i in range(GROUP):
             if (j, i) != (0, 0):
                 e_copies[at].wait_recv()
                 at += 1
-        lines = []
-        for i in range(GROUP):
-            q = peer(j, i, -1)
-            lines.append(jnp.where(slot < counts_ref[0, q], dstrow_ref[pl.ds(q, 1), :], -1))
-        targets = jnp.concatenate(lines, axis=1)
-        onehot = (row_of == targets).astype(BF16)
         projected = dot(incoming[j], wsv[...]).astype(BF16).astype(F32)
-        parts = dot_t(onehot, dsthl[...])
-        gates = 0.5 + 0.5 * jnp.tanh(0.5 * (parts[:, :D] + parts[:, D:] + projected[:, :D]))
+        gates = 0.5 + 0.5 * jnp.tanh(0.5 * (received[j] + projected[:, :D]))
         stacked = jnp.concatenate([gates * projected[:, D:], gates], axis=1).astype(BF16)
-        sums = dot(onehot, stacked)
+        sums = dot(hits[j], stacked)
         if n == 0:
             acc[...] = sums
         else:
             acc[...] += sums
 
     total = base[...] + acc[:, :D] / (1.0 + acc[:, D:])
-    spread = lax.rsqrt(jnp.mean(total * total, axis=1, keepdims=True) + 1e-6)
-    out_ref[...] = (total * spread * gain_ref[...]).astype(BF16)
+    out_ref[...] = total * lax.rsqrt(jnp.mean(total * total, axis=1, keepdims=True) + 1e-6)
 
     for cp in copies:
         cp.wait_send()
@@ -279,16 +303,20 @@
 ):
     hbm = pl.BlockSpec(memory_space=pl.ANY)
     vmem = pl.BlockSpec(memory_space=pltpu.VMEM)
-    smem = pl.BlockSpec(memory_space=pltpu.SMEM)
     dma = pltpu.SemaphoreType.DMA
-    return pl.pallas_call(
+    normalized = pl.pallas_call(
         kernel,
-        out_shape=jax.ShapeDtypeStruct((ROWS, D), BF16),
-        in_specs=[hbm] * 8 + [vmem] * 3 + [smem, vmem],
+        out_shape=jax.ShapeDtypeStruct((ROWS, D), F32),
+        in_specs=[hbm] * 12,
         out_specs=vmem,
         scratch_shapes=[
             pltpu.VMEM((LOOPS, ROWS, D), BF16),
             pltpu.VMEM((LOOPS, 1, ROWS), jnp.int32),
+            pltpu.VMEM((CAP, PEERS), jnp.int32),
+            pltpu.VMEM((CAP, PEERS), jnp.int32),
+            pltpu.SMEM((1, PEERS), jnp.int32),
+            pltpu.VMEM((128, 128), jnp.int32),
+            pltpu.VMEM((128, 128), jnp.int32),
             pltpu.VMEM((D, D), BF16),
             pltpu.VMEM((D, 2 * D), BF16),
             pltpu.VMEM((D, D), BF16),
@@ -298,14 +326,16 @@
             pltpu.VMEM((NZ, SLOTS, D), BF16),
             pltpu.VMEM((NZ, SLOTS, D), BF16),
             pltpu.VMEM((ROWS, 2 * D), BF16),
-            pltpu.VMEM((PAIRS, KEYS, 256), BF16),
+            pltpu.VMEM((NZ, ROWS, SLOTS), BF16),
+            pltpu.VMEM((NZ, SLOTS, D), F32),
+            pltpu.VMEM((PAIRS, 256, KEYS), BF16),
             pltpu.VMEM((PAIRS, KEYS, 256), BF16),
             pltpu.VMEM((PAIRS, ROWS, 128), BF16),
             pltpu.VMEM((ROWS, 128), BF16),
             pltpu.VMEM((PAIRS, ROWS, 128), BF16),
             pltpu.VMEM((ROWS, D), F32),
             pltpu.VMEM((ROWS, 2 * D), F32),
-            dma((8,)),
+            dma((12,)),
             dma((LOOPS,)),
             dma((LOOPS,)),
             dma((LOOPS,)),
@@ -326,12 +356,12 @@
         w_key,
         w_value,
         w_out,
-        norm_gain.reshape(1, D),
-        send_rows.reshape(send_rows.shape[2:]),
-        dst_rows.reshape(dst_rows.shape[2:]),
+        send_rows[0, 0].T,
+        dst_rows[0, 0].T,
         counts.reshape(1, -1),
         batch_ids,
     )
+    return (normalized * norm_gain).astype(BF16)
 
 
 def solution(mesh):

time: 75 us -> 66.7 us (0.89)
  Pallas kernels: 70.8 us -> 64.4 us
  local copies, waits for them, and re-layouts: 3.99 us -> 0.01 us
  other arithmetic: 0 us -> 2.14 us
    pallas_call x1, Pallas kernels: 70.8 us -> 64.4 us  [per_device(): pl.pallas_call(kernel, out_shape=jax.ShapeDtypeStruct((ROWS, D), F32), in...]
    unnamed x5 -> x2, local copies, waits for them, and re-layouts: 3.99 us -> 0.01 us
    convert_element_type x0 -> x1, other arithmetic: none -> 2.14 us  [per_device(): return (normalized * norm_gain).astype(BF16)]
where the time goes in v2:
time: 66.7 us; the launch traced here: 66.6 us
  Pallas kernels  64.4 us (97%)
  other arithmetic  2.14 us (3%)
    pallas_call x1, Pallas kernels, per_device(): pl.pallas_call(kernel, out_shape=jax.ShapeDtypeStruct((ROWS, D), F32), in...  64.4 us
    convert_element_type x1, other arithmetic, per_device(): return (normalized * norm_gain).astype(BF16)  2.14 us

profile of v2, /device:TPU:1, one launch (start us, length us, event | category | flops | bytes accessed | tf_op | source)
XLA Modules:
  0.0 66.6 jit_solution(2763014983428851223)
XLA Ops:
  0.0 0.0 copy-start
  0.0 64.4 %shard_map.127 = f32[512,512]{1,0:T(8,128)} custom-call(bf16[512,512]{1,0:T(8,128)(2,1)} %rows_hbm.1, bf16[512,512]{1,0:T(8,128)(2,1)} %wdst_hbm.1, bf16[512,512]{1,0:T(8,128)(2,1)} %wsrc_hbm.1, bf16[512,512]{1,0:T(8,128)(2,1)} %wval_hbm.1, bf16[512,512]{1,0:T(8,128)(2,1)} %wq_hbm.1, bf16[512,512]{1,0:T(8,128)(2,1)} %wk_hbm.1, bf16[512,512]{1,0:T(8,128)(2,1)} %wv_hbm.1, ...), custom_call_target="tpu_custom_call" | custom-call | flops 14000000000 | bytes 5242880 | tf_op jit(solution)/shard_map/pallas_call | solution.py:307
  64.4 0.0 copy-done
  64.4 2.1 %multiply_convert_fusion = bf16[512,512]{1,0:T(8,128)(2,1)} fusion(f32[512,512]{1,0:T(8,128)} %shard_map.127, f32[512]{0:T(512)S(1)} %copy-done), kind=kLoop, calls=%fused_computation | loop fusion | flops 524288 | bytes 1574912 | tf_op jit(solution)/shard_map/convert_element_type | solution.py:364
Async XLA Ops:
  0.0 64.4 %copy-start = (f32[512]{0:T(512)S(1)}, f32[512]{0:T(512)}, u32[]{:S(2)}) copy-start(f32[512]{0:T(512)} %param.21) | copy-start | bytes 6148

commit v3 on v2

--- a/solution.py
+++ b/solution.py
@@ -18,12 +18,14 @@
 CAP = 32
 LOOPS = 4
 NX, NZ, NC = 4, 8, 2
-GROUP = NX * NC
+GROUP = NZ
 PEERS = NX * NZ * NC
+GROUPS = PEERS // GROUP
 SLOTS = GROUP * CAP
 KEYS = LOOPS * ROWS
 BIG = 1e30
-ORDER = (4, 3, 5, 2, 6, 1, 7, 0)
+STEPS = (4, 3, 5, 2, 6, 1, 7, 0)
+SELF = (1, 7)
 LATER = (1, 3, 2)
 
 
@@ -52,6 +54,7 @@
     dstrow_hbm,
     counts_hbm,
     ids_hbm,
+    gain_ref,
     out_ref,
     rows,
     ids,
@@ -91,10 +94,9 @@
     x, z, c = dom // (NZ * NC), (dom // NC) % NZ, dom % NC
 
     def peer(j, i, sign):
-        dx, dc = i // NC, i % NC
-        px = (x + sign * dx + NX) % NX
-        pz = (z + sign * j + NZ) % NZ
-        pc = (c + dc) % NC
+        px = (x + sign * ((j + i) % NX) + NX) % NX
+        pz = (z + sign * STEPS[i] + NZ) % NZ
+        pc = (c + j // NX) % NC
         return (px * NZ + pz) * NC + pc
 
     loads = [
@@ -122,9 +124,9 @@
     barrier = pltpu.get_barrier_semaphore()
     for k in range(1, LOOPS):
         pl.semaphore_signal(barrier, inc=1, device_id=(dom, (lp + k) % LOOPS), device_id_type=MESH)
-    for j in ORDER:
+    for j in range(GROUPS):
         for i in range(GROUP):
-            if (j, i) != (0, 0):
+            if (j, i) != SELF:
                 pl.semaphore_signal(barrier, inc=1, device_id=(peer(j, i, 1), lp), device_id_type=MESH)
 
     for cp in loads[3:]:
@@ -141,14 +143,15 @@
     row_of = lax.broadcasted_iota(jnp.int32, (ROWS, SLOTS), 0)
 
     copies = []
-    for n, j in enumerate(ORDER):
+    for j in range(GROUPS):
         picks = jnp.concatenate([send_ref[pl.ds(peer(j, i, 1), 1), :CAP] for i in range(GROUP)], axis=1)
         onehot = (row_of == picks).astype(BF16)
         picked = dot_t(onehot, rows[0]).astype(BF16)
+        if j == SELF[0]:
+            own = pl.ds(SELF[1] * CAP, CAP)
+            incoming[j, own, :] = picked[SELF[1] * CAP : (SELF[1] + 1) * CAP]
+        outgoing[j] = picked
         if j == 0:
-            incoming[0, pl.ds(0, CAP), :] = picked[:CAP]
-        outgoing[j] = picked
-        if n == 0:
             pl.semaphore_wait(barrier, LOOPS - 1 + NX * NZ * NC - 1)
             for k in LATER:
                 to = (dom, (lp + k) % LOOPS)
@@ -167,7 +170,7 @@
                     cp.start()
                     copies.append(cp)
         for i in range(GROUP):
-            if (j, i) == (0, 0):
+            if (j, i) == SELF:
                 continue
             cp = pltpu.make_async_remote_copy(
                 src_ref=outgoing.at[j, pl.ds(i * CAP, CAP)],
@@ -234,7 +237,7 @@
         received[j] = parts[:, :D] + parts[:, D:]
         return carry
 
-    lax.fori_loop(0, NZ, targets_of, 0)
+    lax.fori_loop(0, GROUPS, targets_of, 0)
     project(0, 0)
     for n, k in enumerate(LATER):
         y_copies[2 * n].wait_recv()
@@ -265,22 +268,23 @@
     loads[9].wait()
     loads[10].wait()
     at = 0
-    for n, j in enumerate(ORDER):
+    for j in range(GROUPS):
         for i in range(GROUP):
-            if (j, i) != (0, 0):
+            if (j, i) != SELF:
                 e_copies[at].wait_recv()
                 at += 1
         projected = dot(incoming[j], wsv[...]).astype(BF16).astype(F32)
         gates = 0.5 + 0.5 * jnp.tanh(0.5 * (received[j] + projected[:, :D]))
         stacked = jnp.concatenate([gates * projected[:, D:], gates], axis=1).astype(BF16)
         sums = dot(hits[j], stacked)
-        if n == 0:
+        if j == 0:
             acc[...] = sums
         else:
             acc[...] += sums
 
     total = base[...] + acc[:, :D] / (1.0 + acc[:, D:])
-    out_ref[...] = total * lax.rsqrt(jnp.mean(total * total, axis=1, keepdims=True) + 1e-6)
+    normed = total * lax.rsqrt(jnp.mean(total * total, axis=1, keepdims=True) + 1e-6)
+    out_ref[...] = (normed * gain_ref[...]).astype(BF16)
 
     for cp in copies:
         cp.wait_send()
@@ -306,8 +310,8 @@
     dma = pltpu.SemaphoreType.DMA
     normalized = pl.pallas_call(
         kernel,
-        out_shape=jax.ShapeDtypeStruct((ROWS, D), F32),
-        in_specs=[hbm] * 12,
+        out_shape=jax.ShapeDtypeStruct((ROWS, D), BF16),
+        in_specs=[hbm] * 12 + [vmem],
         out_specs=vmem,
         scratch_shapes=[
             pltpu.VMEM((LOOPS, ROWS, D), BF16),
@@ -323,11 +327,11 @@
             pltpu.VMEM((D, D), BF16),
             pltpu.VMEM((D, D), BF16),
             pltpu.VMEM((D, D), BF16),
-            pltpu.VMEM((NZ, SLOTS, D), BF16),
-            pltpu.VMEM((NZ, SLOTS, D), BF16),
+            pltpu.VMEM((GROUPS, SLOTS, D), BF16),
+            pltpu.VMEM((GROUPS, SLOTS, D), BF16),
             pltpu.VMEM((ROWS, 2 * D), BF16),
-            pltpu.VMEM((NZ, ROWS, SLOTS), BF16),
-            pltpu.VMEM((NZ, SLOTS, D), F32),
+            pltpu.VMEM((GROUPS, ROWS, SLOTS), BF16),
+            pltpu.VMEM((GROUPS, SLOTS, D), F32),
             pltpu.VMEM((PAIRS, 256, KEYS), BF16),
             pltpu.VMEM((PAIRS, KEYS, 256), BF16),
             pltpu.VMEM((PAIRS, ROWS, 128), BF16),
@@ -340,8 +344,8 @@
             dma((LOOPS,)),
             dma((LOOPS,)),
             dma((LOOPS,)),
-            dma((NZ, GROUP)),
-            dma((NZ, GROUP)),
+            dma((GROUPS, GROUP)),
+            dma((GROUPS, GROUP)),
         ],
         compiler_params=pltpu.CompilerParams(
             collective_id=0, has_side_effects=True, vmem_limit_bytes=56 * 2**20
@@ -360,8 +364,9 @@
         dst_rows[0, 0].T,
         counts.reshape(1, -1),
         batch_ids,
+        norm_gain.reshape(1, D),
     )
-    return (normalized * norm_gain).astype(BF16)
+    return normalized
 
 
 def solution(mesh):

time: 66.7 us -> 66.3 us (level)
  other arithmetic: 2.14 us -> 0 us
  local copies, waits for them, and re-layouts: 0.01 us -> 1.87 us
    convert_element_type x1 -> x0, other arithmetic: 2.14 us -> none  [per_device(): return (normalized * norm_gain).astype(BF16)]
    unnamed x2 -> x1, local copies, waits for them, and re-layouts: 0.01 us -> 1.87 us
where the time goes in v3:
time: 66.3 us; the launch traced here: 66.1 us
  Pallas kernels  64.2 us (97%)
  local copies, waits for them, and re-layouts  1.87 us (3%)
    pallas_call x1, Pallas kernels, per_device(): pl.pallas_call(kernel, out_shape=jax.ShapeDtypeStruct((ROWS, D), BF16), i...  64.2 us
    unnamed x1, local copies, waits for them, and re-layouts  1.87 us

profile of v3, /device:TPU:1, one launch (start us, length us, event | category | flops | bytes accessed | tf_op | source)
XLA Modules:
  0.0 66.1 jit_solution(6014796345177627318)
XLA Ops:
  0.0 64.2 %shard_map.127 = bf16[512,512]{1,0:T(8,128)(2,1)} custom-call(bf16[512,512]{1,0:T(8,128)(2,1)} %rows_hbm.1, bf16[512,512]{1,0:T(8,128)(2,1)} %wdst_hbm.1, bf16[512,512]{1,0:T(8,128)(2,1)} %wsrc_hbm.1, bf16[512,512]{1,0:T(8,128)(2,1)} %wval_hbm.1, bf16[512,512]{1,0:T(8,128)(2,1)} %wq_hbm.1, bf16[512,512]{1,0:T(8,128)(2,1)} %wk_hbm.1, ...), custom_call_target="tpu_custom_call" | custom-call | flops 14000000000 | bytes 5242880 | tf_op jit(solution)/shard_map/pallas_call | solution.py:311
  64.2 1.9 %copy.15 = bf16[512,512]{1,0:T(8,128)(2,1)} copy(bf16[512,512]{1,0:T(8,128)(2,1)} %shard_map.127) | data formatting | bytes 1048576
